TPU v7x, 32 devices: a whole 2x2x4 slice. The times are simulated.
32 devices in a mesh: row: 2 (over core), col: 4 (over y, x), inner: 4 (over z).
Axes of the slice: x: 2, y: 2, z: 4, core: 2. Of those that a mesh axis runs over, the one named last changes fastest.
Arguments:
- density: bfloat16 [64, 16, 256, 256], P('row', ('col', 'inner')), may hold values from -1.5 to 1.5, as said below
- block_cols: int32 [64, 16], replicated, may hold values from 0 to 63, as said below
- mixing: float32 [3], replicated, may hold values from 0.02 to 1.5, as said below
Outputs:
- purified: bfloat16 [64, 16, 256, 256], P('row', ('col', 'inner'))
Inputs may be any that keep to these rules, and one draw needn't show every extreme that they name: Slot g of block row i names a block row of group g (rows g * 4 to g * 4 + 3); within one group of block rows, slot g names each row of group g once. Slot i // 4 of row i names i itself. The pattern is symmetric: row block_cols[i, g] names i in slot i // 4. It is consistent: block_cols[block_cols[i, t], g] == block_cols[i, g] for all i, t, g. `density`: block (i, g) is the transpose of block (block_cols[i, g], i // 4). `mixing`: element 0 lies in 0.5 to 1.5, elements 1 and 2 in 0.02 to 0.05.
All inputs are finite; a program needn't handle non-finite values.
Results may differ from a plain program's by a relative error of at most 0.007.
Values may be sent and summed in bfloat16 or wider, within the bound.
A program may use at most 128 MiB of HBM per device.

v0:
```python
import jax
import jax.numpy as jnp
from jax import lax
from jax.sharding import PartitionSpec as P

GS = 4


def fold_with(panel, piece):
    return jnp.einsum("htab,tgbc->hgac", panel, piece, preferred_element_type=jnp.float32)


def clique_filter(density, block_cols, mixing, row_start):
    row_count = density.shape[0]
    width = density.shape[2]
    groups_here = row_count // GS
    first_group = row_start // GS
    leaders = lax.dynamic_slice_in_dim(block_cols[:GS], first_group, groups_here, 1)
    ordered = density[:, 0][(leaders - row_start).reshape(-1)]
    ordered = ordered.reshape(GS, groups_here, 1, width, width)
    arrived = lax.all_to_all(ordered, "inner", split_axis=0, concat_axis=2, tiled=True)
    blocks = arrived[0]
    slot_count = blocks.shape[1]
    slot_start = lax.axis_index("col") * slot_count
    density_panel = lax.all_gather(blocks, "col", axis=1, tiled=True)
    square = fold_with(density_panel, lax.all_gather(blocks, "row", axis=0, tiled=True)).astype(
        jnp.bfloat16
    )
    group_ids = first_group + jnp.arange(groups_here, dtype=jnp.int32)
    slot_ids = slot_start + jnp.arange(slot_count, dtype=jnp.int32)
    on_diagonal = (group_ids[:, None] == slot_ids[None, :]).astype(jnp.float32)
    identity = jnp.eye(width, dtype=jnp.float32)
    mixer_blocks = (
        mixing[0] * on_diagonal[:, :, None, None] * identity
        + mixing[1] * blocks.astype(jnp.float32)
        + mixing[2] * square.astype(jnp.float32)
    ).astype(jnp.bfloat16)
    square_panel = lax.all_gather(square, "col", axis=1, tiled=True)
    filtered = fold_with(
        square_panel, lax.all_gather(mixer_blocks, "row", axis=0, tiled=True)
    ).astype(jnp.bfloat16)
    returned = lax.all_to_all(filtered[None], "inner", split_axis=2, concat_axis=0, tiled=True)
    regrouped = returned.reshape(GS * groups_here, 1, width, width)
    local_rows = row_start + jnp.arange(row_count, dtype=jnp.int32)
    clique_ids = lax.dynamic_slice_in_dim(block_cols[:, 0], row_start, row_count, 0)
    positions = clique_ids * groups_here + (local_rows // GS - first_group)
    return regrouped[positions]


def body(density, block_cols, mixing):
    row_count = density.shape[0]
    row_start = lax.axis_index("row") * row_count
    return clique_filter(density, block_cols, mixing, row_start)


def solution(mesh):
    in_specs = (P("row", ("col", "inner"), None, None), P(), P())
    out_specs = P("row", ("col", "inner"), None, None)
    return jax.shard_map(body, mesh=mesh, in_specs=in_specs, out_specs=out_specs, check_vma=False)
```

profile of v0, /device:TPU:12, one launch (start us, length us, event | category | flops | bytes accessed | tf_op | source)
XLA Modules:
  0.0 637.9 jit_solution(16460091257563989549)
XLA Ops:
  6.5 0.0 all-gather.11.cloned.1.call-start
  6.5 0.7 dynamic-slice_subtract_fusion
  7.2 0.1 copy.15
  7.3 0.1 reshape.140
  7.4 5.0 gather_fusion
  12.4 96.6 %all_to_all.30 = bf16[4,8,1,256,256]{4,3,1,2,0:T(8,128)(2,1)S(1)} all-to-all(bf16[4,8,1,256,256]{4,3,1,2,0:T(8,128)(2,1)} %bitcast.84), channel_id=1, replica_groups=mesh['row'=2,'col'=4,'inner'=4] {'inner'}, dimensions={0} | all-to-all | bytes 8388608 | tf_op jit(solution)/shard_map/all_to_all | solution.py:21
  109.1 0.0 copy-start
  109.1 2.0 copy-done
  111.1 2.3 copy.40
  113.4 0.0 all-gather.11.cloned.1.call-update
  113.5 0.0 all-gather.13.cloned.1.call-start
  113.5 0.7 all-gather.13.cloned.1.call-update
  114.2 0.0 all-gather.7.cloned.1.call-start
  114.3 0.0 copy-done.1
  114.3 0.6 fusion.21
  114.9 0.7 compare_select_fusion
  115.7 18.7 %all-gather.11.cloned.1.call-done = bf16[1,16,4,1,256,256]{5,4,3,2,0,1:T(8,128)(2,1)} async-done(((bf16[1,8,4,1,256,256]{5,4,3,2,0,1:T(8,128)(2,1)}), bf16[1,16,4,1,256,256]{5,4,3,2,0,1:T(8,128)(2,1)}) %all-gather.11.cloned.1.call-update) | async-done | bytes 8388624 | tf_op jit(solution)/shard_map/all_gather | solution.py:26
  134.3 11.5 %copy.19 = bf16[1,16,4,1,256,256]{4,5,1,2,3,0:T(8,128)(2,1)} copy(bf16[1,16,4,1,256,256]{5,4,3,2,0,1:T(8,128)(2,1)} %all-gather.11.cloned.1.call-done) | data formatting | bytes 16777216 | tf_op jit(solution)/shard_map/all_gather | solution.py:26
  145.9 148.7 %all-gather.13.cloned.1.call-done = bf16[1,8,16,1,256,256]{5,4,2,1,3,0:T(8,128)(2,1)} async-done(((bf16[1,8,4,1,256,256]{5,4,2,1,3,0:T(8,128)(2,1)}), bf16[1,8,16,1,256,256]{5,4,2,1,3,0:T(8,128)(2,1)}) %all-gather.13.cloned.1.call-update) | async-done | bytes 16777232 | tf_op jit(solution)/shard_map/all_gather | solution.py:25
  294.5 25.9 %fusion.7 = (bf16[8,4,256,256]{3,2,1,0:T(8,128)(2,1)}, bf16[8,4,256,256]{3,2,1,0:T(8,128)(2,1)}) fusion(f32[]{:T(128)} %bitcast.1, f32[]{:T(128)} %bitcast.9, f32[256,256]{1,0:T(8,128)S(1)} %fusion.18, f32[8,4]{1,0:T(8,128)S(1)} %compare_select_fusion, bf16[4,8,1,256,256]{4,3,1,2,0:T(8,128)(2,1)} %copy-done, ...), kind=kOutput, calls=%fused_computation.12 | convolution fusion | flops 17198743552 | bytes 38011016 | tf_op jit(solution)/shard_map/htab,tgbc->hgac/dot_general | solution.py:10
  320.4 0.0 all-gather.7.cloned.1.call-update
  320.4 0.0 all-gather.9.cloned.1.call-start
  320.5 0.5 all-gather.9.cloned.1.call-update
  321.0 19.7 %all-gather.7.cloned.1.call-done = bf16[16,4,256,256]{3,2,1,0:T(8,128)(2,1)} async-done(((bf16[8,4,256,256]{3,2,1,0:T(8,128)(2,1)}), bf16[16,4,256,256]{3,2,1,0:T(8,128)(2,1)}) %all-gather.7.cloned.1.call-update) | async-done | bytes 8388624 | tf_op jit(solution)/shard_map/all_gather | solution.py:40
  340.7 160.1 %all-gather.9.cloned.1.call-done = bf16[8,16,256,256]{3,2,1,0:T(8,128)(2,1)} async-done(((bf16[8,4,256,256]{3,2,1,0:T(8,128)(2,1)}), bf16[8,16,256,256]{3,2,1,0:T(8,128)(2,1)}) %all-gather.9.cloned.1.call-update) | async-done | bytes 16777232 | tf_op jit(solution)/shard_map/all_gather | solution.py:38
  500.8 23.8 %fusion.9 = bf16[1,8,4,256,256]{3,4,1,0,2:T(8,128)(2,1)} fusion(bf16[8,16,256,256]{3,2,1,0:T(8,128)(2,1)} %all-gather.9.cloned.1.call-done, bf16[16,4,256,256]{3,2,1,0:T(8,128)(2,1)} %all-gather.7.cloned.1.call-done), kind=kOutput, calls=%fused_computation.14 | convolution fusion | flops 17181966336 | bytes 29360128 | tf_op jit(solution)/shard_map/htab,tgbc->hgac/dot_general | solution.py:10
  524.6 5.4 all-to-all-start.1
  530.0 0.7 slice.19
  530.7 0.1 fusion.20
  530.7 89.4 %all-to-all-done.1 = bf16[1,8,4,256,256]{3,4,1,0,2:T(8,128)(2,1)} async-done(((bf16[1,8,4,256,256]{3,4,1,0,2:T(8,128)(2,1)}), bf16[1,8,4,256,256]{3,4,1,0,2:T(8,128)(2,1)}, u32[]{:S(2)}, u32[]{:S(2)}) %all-to-all-start.1) | async-done | bytes 4194336 | tf_op jit(solution)/shard_map/all_to_all | solution.py:42
  620.1 6.2 copy.23
  626.4 5.0 gather_fusion.1
  (7 shorter events, 0.1 us)
Async XLA Ops:
  6.5 127.8 %all-gather.11.cloned.1.call-start = ((), (), s32[]{:S(2)}) async-start(), calls=%async_computation.4 | async-start | bytes 12582912 | tf_op jit(solution)/shard_map/all_gather | solution.py:26
  109.1 2.0 copy-start
  111.1 3.2 copy-start.1
  113.5 181.1 %all-gather.13.cloned.1.call-start = ((), (), s32[]{:S(2)}) async-start(), calls=%async_computation.5 | async-start | bytes 20971520 | tf_op jit(solution)/shard_map/all_gather | solution.py:25
  114.2 226.5 %all-gather.7.cloned.1.call-start = ((), (), s32[]{:S(2)}) async-start(), calls=%async_computation.2 | async-start | bytes 12582912 | tf_op jit(solution)/shard_map/all_gather | solution.py:40
  320.4 180.3 %all-gather.9.cloned.1.call-start = ((), (), s32[]{:S(2)}) async-start(), calls=%async_computation.3 | async-start | bytes 20971520 | tf_op jit(solution)/shard_map/all_gather | solution.py:38
  524.6 95.5 %all-to-all-start.1 = ((bf16[1,8,4,256,256]{3,4,1,0,2:T(8,128)(2,1)}), bf16[1,8,4,256,256]{3,4,1,0,2:T(8,128)(2,1)}, u32[]{:S(2)}, u32[]{:S(2)}) async-start(bf16[1,8,4,256,256]{3,4,1,0,2:T(8,128)(2,1)} %fusion.9), calls=%async_computation.1 | async-start | bytes 8388608 | tf_op jit(solution)/shard_map/all_to_all | solution.py:42
Sparse Core Ops, SparseCore 0:
  113.6 20.7 all-gather.10
  136.2 158.3 all-gather.12
  320.6 20.1 all-gather.6
  342.4 158.3 all-gather.8
where the time goes:
time: 643 us; the launch traced here: 638 us
  waiting for transfers between devices  438 us (68%)
  blocking collectives  96.6 us (15%)
  matrix products  49.7 us (8%)
  local copies, waits for them, and re-layouts  33.6 us (5%)
  between operations  13.2 us (2%)
    all_gather x1, waiting for transfers between devices, clique_filter(): square_panel = lax.all_gather(square, 'col', axis=1, tiled=True)  160 us
    all_gather x1, waiting for transfers between devices, clique_filter(): density_panel = lax.all_gather(blocks, 'col', axis=1, tiled=True)  149 us
    all_to_all x1, blocking collectives, clique_filter(): lax.all_to_all(ordered, 'inner', split_axis=0, concat_axis=2, tiled=True)  96.6 us
    all_to_all x1, waiting for transfers between devices, clique_filter(): lax.all_to_all(filtered[None], 'inner', split_axis=2, concat_axis=0, tile...  89.4 us
    dot_general x2, matrix products, fold_with(): jnp.einsum('htab,tgbc->hgac', panel, piece, preferred_element_type=jnp.fl...  49.7 us
    all_gather x1, waiting for transfers between devices, clique_filter(): lax.all_gather(mixer_blocks, 'row', axis=0, tiled=True)  19.7 us
    all_gather x1, waiting for transfers between devices, clique_filter(): lax.all_gather(blocks, 'row', axis=0, tiled=True)  18.7 us
  transfers between devices with their start and end apart: 5, of which 5 were waited for; matrix products, arithmetic and copies ran while one was open for 2% of the time, Pallas kernels for 0%

commit v1 on v0

--- a/solution.py
+++ b/solution.py
@@ -1,6 +1,10 @@
+import functools
+
 import jax
 import jax.numpy as jnp
 from jax import lax
+from jax.experimental import pallas as pl
+from jax.experimental.pallas import tpu as pltpu
 from jax.sharding import PartitionSpec as P
 
 GS = 4
@@ -47,13 +51,344 @@
     return regrouped[positions]
 
 
-def body(density, block_cols, mixing):
+def product_kernel(
+    slots, half, width, mixing_ref, ordered_ref, out_ref,
+    left, own, oth, xo, yn, dt, own2, oth2, xo2, yn2, dt2,
+    z_send, z_recv, in_sem, send_sems, recv_sems, p_send, p_recv, out_sem,
+):
+    tile = half // 2
+    rows = half * width
+    r = lax.axis_index("row")
+    c = lax.axis_index("col")
+    z = lax.axis_index("inner")
+    y, x = c // 2, c % 2
+    to_x = {"col": y * 2 + (1 - x)}
+    to_y = {"col": (1 - y) * 2 + x}
+    to_core = {"row": 1 - r}
+    base0 = x * tile
+    base1 = (1 - x) * tile
+    diag = r == y
+    MESH = pl.DeviceIdType.MESH
+
+    def others(k):
+        return (z + k) % slots
+
+    barrier = pltpu.get_barrier_semaphore()
+    for k in range(1, slots):
+        pl.semaphore_signal(barrier, inc=1, device_id={"inner": others(k)}, device_id_type=MESH)
+    for target in (to_x, to_y, to_core):
+        pl.semaphore_signal(barrier, inc=1, device_id=target, device_id_type=MESH)
+    pl.semaphore_wait(barrier, slots - 1 + 3)
+
+    def remote(src, dst, send, recv, target):
+        return pltpu.make_async_remote_copy(
+            src_ref=src, dst_ref=dst, send_sem=send, recv_sem=recv, device_id=target, device_id_type=MESH
+        )
+
+    def z_copy(k):
+        to = others(k)
+        return remote(ordered_ref.at[to], own.at[z], z_send.at[k], z_recv.at[z], {"inner": to})
+
+    def z_arrival(s):
+        return remote(ordered_ref.at[s], own.at[s], z_send.at[0], z_recv.at[s], {"inner": s})
+
+    for k in range(1, slots):
+        z_copy(k).start()
+    keep = pltpu.make_async_copy(ordered_ref.at[z], own.at[z], in_sem)
+    keep.start()
+
+    def links(phase):
+        mine, oth_, xo_, yn_, dt_ = ((own, oth, xo, yn, dt), (own2, oth2, xo2, yn2, dt2))[phase]
+        diag_rows = pl.ds(pl.multiple_of(base0 * width, width), tile * width)
+
+        def make(kind, index, src, dst, target):
+            return lambda s: remote(
+                src(s), dst.at[s], send_sems.at[phase, index, s], recv_sems.at[phase, kind, s], target
+            )
+
+        return dict(
+            core=make(0, 0, lambda s: mine.at[s], oth_, to_core),
+            xo=make(1, 1, lambda s: mine.at[s], xo_, to_x),
+            yn=make(2, 2, lambda s: mine.at[s], yn_, to_y),
+            dt=make(3, 3, lambda s: mine.at[s, diag_rows], dt_, to_x),
+            dt_y=make(3, 1, lambda s: dt_.at[s], dt_, to_y),
+            xo_relay=make(1, 2, lambda s: xo_.at[s], xo_, to_core),
+        )
+
+    def send_first(link, s):
+        @pl.when(diag)
+        def _():
+            link["yn"](s).start()
+            link["dt"](s).start()
+            link["core"](s).start()
+
+        @pl.when(jnp.logical_not(diag))
+        def _():
+            link["xo"](s).start()
+            link["core"](s).start()
+
+    def wait_sends(link, s):
+        @pl.when(diag)
+        def _():
+            for name in ("yn", "dt", "core", "dt_y"):
+                link[name](s).wait_send()
+
+        @pl.when(jnp.logical_not(diag))
+        def _():
+            for name in ("xo", "core", "xo_relay"):
+                link[name](s).wait_send()
+
+    def relay_dt(link, s):
+        link["dt"](s).wait_recv()
+        link["dt_y"](s).start()
+
+    def relay_xo(link, s):
+        link["xo"](s).wait_recv()
+        link["xo_relay"](s).start()
+
+    def group(g):
+        return pl.ds(pl.multiple_of(g * width, width), width)
+
+    def put_same(source, s):
+        def step(g, carry):
+            left[base0 + s, group(g), :] = source[s, group(g), :]
+            return carry
+        lax.fori_loop(0, half, step, 0)
+
+        def flip(g, carry):
+            left[base1 + g, group(base0 + s), :] = source[s, group(base1 + g), :].T
+            return carry
+        lax.fori_loop(0, tile, flip, 0)
+
+    def put_dt(source, s):
+        def step(g, carry):
+            left[base1 + s, group(base1 + g), :] = source[s, group(g), :]
+            return carry
+        lax.fori_loop(0, tile, step, 0)
+
+    def put_flipped(source, s, base):
+        def step(g, carry):
+            left[half + g, group(base + s), :] = source[s, group(g), :].T
+            return carry
+        lax.fori_loop(0, half, step, 0)
+
+    def put_plain(source, s, base):
+        def step(g, carry):
+            left[half + base + s, group(g), :] = source[s, group(g), :]
+            return carry
+        lax.fori_loop(0, half, step, 0)
+
+    chunk = rows // 4
+
+    def multiply(right0, right1, s, row_start):
+        here = pl.ds(pl.multiple_of(row_start, chunk), chunk)
+        lhs = jnp.concatenate([left[k, here, :] for k in range(2 * half)], axis=1)
+        rhs = jnp.concatenate([right0[s], right1[s]], axis=0)
+        return jnp.dot(lhs, rhs, preferred_element_type=jnp.float32).astype(jnp.bfloat16)
+
+    link = links(0)
+    order = [z, z + 1 - 2 * (z % 2), (z + 2) % 4, 3 - z] if slots == 4 else [others(k) for k in range(slots)]
+
+    def relay_and_put(s):
+        @pl.when(diag)
+        def _():
+            relay_dt(link, s)
+            put_same(own, s)
+            put_dt(dt, s)
+            link["core"](s).wait_recv()
+            put_flipped(oth, s, base0)
+            link["xo_relay"](s).wait_recv()
+            put_flipped(xo, s, base1)
+
+        @pl.when(jnp.logical_not(diag))
+        def _():
+            relay_xo(link, s)
+            put_plain(own, s, base0)
+            put_plain(xo, s, base1)
+            link["yn"](s).wait_recv()
+            put_same(yn, s)
+            link["dt_y"](s).wait_recv()
+            put_dt(dt, s)
+            link["core"](s).wait_recv()
+
+    for k, s in enumerate(order):
+        if k == 0:
+            keep.wait()
+        else:
+            z_arrival(s).wait_recv()
+        send_first(link, s)
+        if k:
+            relay_and_put(order[k - 1])
+    relay_and_put(order[-1])
+
+    link2 = links(1)
+
+    def square_slot(s, carry):
+        def step(m, carry):
+            here = pl.ds(pl.multiple_of(m * chunk, chunk), chunk)
+            own2[s, here, :] = multiply(own, oth, s, m * chunk)
+            return carry
+        lax.fori_loop(0, rows // chunk, step, 0)
+        send_first(link2, s)
+        return carry
+
+    lax.fori_loop(0, slots, square_slot, 0)
+
+    for k in range(1, slots):
+        z_copy(k).wait_send()
+    for s in range(slots):
+        wait_sends(link, s)
+
+    a, b, q = mixing_ref[0], mixing_ref[1], mixing_ref[2]
+    eye = (
+        lax.broadcasted_iota(jnp.int32, (width, width), 0) == lax.broadcasted_iota(jnp.int32, (width, width), 1)
+    ).astype(jnp.float32)
+
+    def mix(dense, square, s, holds_diag):
+        def step(g, carry):
+            scale = jnp.where(jnp.logical_and(holds_diag, g == base0 + s), a, 0.0)
+            dense[s, group(g), :] = (
+                scale * eye
+                + b * dense[s, group(g), :].astype(jnp.float32)
+                + q * square[s, group(g), :].astype(jnp.float32)
+            ).astype(jnp.bfloat16)
+            return carry
+        lax.fori_loop(0, half, step, 0)
+
+    for s in range(slots):
+        mix(own, own2, s, diag)
+    for s in range(slots):
+        link2["core"](s).wait_recv()
+        mix(oth, oth2, s, jnp.logical_not(diag))
+
+    staged = yn
+    n_chunk = rows // chunk
+
+    def back(s, m):
+        here = pl.ds(pl.multiple_of(m * chunk, chunk), chunk)
+        return remote(
+            staged.at[s, here], out_ref.at[z, here], p_send.at[s, m], p_recv.at[z, m], {"inner": s}
+        )
+
+    def back_arrival(s, m):
+        here = pl.ds(pl.multiple_of(m * chunk, chunk), chunk)
+        return remote(
+            staged.at[s, here], out_ref.at[s, here], p_send.at[s, m], p_recv.at[s, m], {"inner": s}
+        )
+
+    def back_here(m):
+        here = pl.ds(pl.multiple_of(m * chunk, chunk), chunk)
+        return pltpu.make_async_copy(staged.at[z, here], out_ref.at[z, here], out_sem.at[m])
+
+    def filter_tile(base):
+        first = base // (half // n_chunk)
+
+        def step(i, carry):
+            m = first + i // slots
+            s = i % slots
+            here = pl.ds(pl.multiple_of(m * chunk, chunk), chunk)
+            staged[s, here, :] = multiply(own, oth, s, m * chunk)
+
+            @pl.when(s == z)
+            def _():
+                back_here(m).start()
+
+            @pl.when(s != z)
+            def _():
+                back(s, m).start()
+            return carry
+        lax.fori_loop(0, (n_chunk // 2) * slots, step, 0)
+
+    @pl.when(diag)
+    def _():
+        for s in range(slots):
+            put_same(own2, s)
+            put_flipped(oth2, s, base0)
+        filter_tile(base0)
+        for s in range(slots):
+            relay_dt(link2, s)
+            put_dt(dt2, s)
+        for s in range(slots):
+            link2["xo_relay"](s).wait_recv()
+            put_flipped(xo2, s, base1)
+        filter_tile(base1)
+
+    @pl.when(jnp.logical_not(diag))
+    def _():
+        for s in range(slots):
+            put_plain(own2, s, base0)
+        for s in range(slots):
+            relay_xo(link2, s)
+            put_plain(xo2, s, base1)
+        for s in range(slots):
+            link2["yn"](s).wait_recv()
+            put_same(yn2, s)
+        filter_tile(base0)
+        for s in range(slots):
+            link2["dt_y"](s).wait_recv()
+            put_dt(dt2, s)
+        filter_tile(base1)
+
+    for s in range(slots):
+        wait_sends(link2, s)
+    for m in range(n_chunk):
+        back_here(m).wait()
+        for k in range(1, slots):
+            back(others(k), m).wait_send()
+        for k in range(1, slots):
+            back_arrival(others(k), m).wait_recv()
+
+
+def plane_filter(density, block_cols, mixing, row_start):
+    row_count = density.shape[0]
+    width = density.shape[2]
+    slots = GS
+    half = row_count // GS
+    first_group = row_start // GS
+    leaders = lax.dynamic_slice_in_dim(block_cols[:GS], first_group, half, 1)
+    ordered = density[:, 0][(leaders - row_start).reshape(-1)]
+    ordered = ordered.reshape(GS, half * width, width)
+    rows = half * width
+    panel = pltpu.VMEM((slots, rows, width), jnp.bfloat16)
+    part = pltpu.VMEM((slots, rows // 2, width), jnp.bfloat16)
+    dma = pltpu.SemaphoreType.DMA
+    returned = pl.pallas_call(
+        functools.partial(product_kernel, slots, half, width),
+        out_shape=jax.ShapeDtypeStruct((slots, rows, width), jnp.bfloat16),
+        in_specs=[pl.BlockSpec(memory_space=pltpu.SMEM), pl.BlockSpec(memory_space=pl.ANY)],
+        out_specs=pl.BlockSpec(memory_space=pl.ANY),
+        scratch_shapes=[
+            pltpu.VMEM((2 * half, rows, width), jnp.bfloat16),
+            panel, panel, panel, panel, part,
+            panel, panel, panel, panel, part,
+            dma((slots,)), dma((slots,)), dma, dma((2, 4, slots)), dma((2, 4, slots)),
+            dma((slots, 4)), dma((slots, 4)), dma((4,)),
+        ],
+        compiler_params=pltpu.CompilerParams(
+            collective_id=0, has_side_effects=True, vmem_limit_bytes=60 * 1024 * 1024
+        ),
+        cost_estimate=pl.CostEstimate(
+            flops=8 * rows * rows * 2 * slots * width, bytes_accessed=4 * slots * rows * width, transcendentals=0
+        ),
+    )(mixing, ordered)
+    regrouped = returned.reshape(GS * half, 1, width, width)
+    local_rows = row_start + jnp.arange(row_count, dtype=jnp.int32)
+    clique_ids = lax.dynamic_slice_in_dim(block_cols[:, 0], row_start, row_count, 0)
+    positions = clique_ids * half + (local_rows // GS - first_group)
+    return regrouped[positions]
+
+
+def body(form, density, block_cols, mixing):
     row_count = density.shape[0]
     row_start = lax.axis_index("row") * row_count
-    return clique_filter(density, block_cols, mixing, row_start)
+    return form(density, block_cols, mixing, row_start)
 
 
 def solution(mesh):
     in_specs = (P("row", ("col", "inner"), None, None), P(), P())
     out_specs = P("row", ("col", "inner"), None, None)
-    return jax.shard_map(body, mesh=mesh, in_specs=in_specs, out_specs=out_specs, check_vma=False)
+    by_plane = mesh.shape["row"] == 2 and mesh.shape["col"] == 4 and mesh.shape["inner"] == GS
+    form = plane_filter if by_plane else clique_filter
+    return jax.shard_map(
+        functools.partial(body, form), mesh=mesh, in_specs=in_specs, out_specs=out_specs, check_vma=False
+    )

time: 643 us -> 290 us (0.45)
  waiting for transfers between devices: 438 us -> 0 us
  Pallas kernels: 0 us -> 278 us
  blocking collectives: 96.6 us -> 0 us
  matrix products: 49.7 us -> 0 us
  local copies, waits for them, and re-layouts: 33.6 us -> 10.9 us
  between operations: 13.2 us -> 0.02 us
    all_gather x4 -> x0, waiting for transfers between devices: 347 us -> none  [the longest x1 160 us: clique_filter(): square_panel = lax.all_gather(square, 'col', axis=1, tiled=True)]
    pallas_call x0 -> x1, Pallas kernels: none -> 278 us  [plane_filter(): pl.pallas_call(functools.partial(product_kernel, slots, half, width), out...]
    all_to_all x1 -> x0, blocking collectives: 96.6 us -> none  [clique_filter(): lax.all_to_all(ordered, 'inner', split_axis=0, concat_axis=2, tiled=True)]
    all_to_all x1 -> x0, waiting for transfers between devices: 89.4 us -> none  [clique_filter(): lax.all_to_all(filtered[None], 'inner', split_axis=2, concat_axis=0, tile...]
    dot_general x2 -> x0, matrix products: 49.7 us -> none  [fold_with(): jnp.einsum('htab,tgbc->hgac', panel, piece, preferred_element_type=jnp.fl...]
    all_gather x1 -> x0, local copies, waits for them, and re-layouts: 11.5 us -> none  [clique_filter(): lax.all_gather(blocks, 'row', axis=0, tiled=True)]
    all_to_all x2 -> x0, local copies, waits for them, and re-layouts: 8.59 us -> none  [the longest x1 6.24 us: clique_filter(): lax.all_to_all(filtered[None], 'inner', split_axis=2, concat_axis=0, tile...]
  transfers between devices with their start and end apart: 5 -> 0, of which waited for: 5 -> 0; matrix products, arithmetic and copies ran while one was open for 2% -> 0% of each run, Pallas kernels for 0% -> 0%
where the time goes in v1:
time: 290 us; the launch traced here: 289 us
  Pallas kernels  278 us (96%)
  local copies, waits for them, and re-layouts  10.9 us (4%)
    pallas_call x1, Pallas kernels, plane_filter(): pl.pallas_call(functools.partial(product_kernel, slots, half, width), out...  278 us

profile of v1, /device:TPU:12, one launch (start us, length us, event | category | flops | bytes accessed | tf_op | source)
XLA Modules:
  0.0 289.2 jit_solution(3641091477920608873)
XLA Ops:
  0.0 0.7 slice.7
  0.7 0.7 dynamic-slice_subtract_fusion
  1.4 0.1 copy.4
  1.5 0.1 reshape.93
  1.6 0.1 fusion
  1.7 5.0 %gather_fusion = bf16[32,256,256]{2,1,0:T(8,128)(2,1)} fusion(bf16[32,256,256]{2,1,0:T(8,128)(2,1)} %bitcast.9, s32[1024]{0:T(1024)S(1)} %pad_clamp_fusion.1), kind=kCustom, calls=%fused_computation | custom fusion | bytes 8388736 | tf_op jit(solution)/shard_map/gather | solution.py:349
  6.7 277.5 %shard_map.37 = bf16[4,2048,256]{2,1,0:T(8,128)(2,1)} custom-call(f32[3]{0:T(128)} %mixing_ref.1, bf16[4,2048,256]{2,1,0:T(8,128)(2,1)} %bitcast.11), custom_call_target="tpu_custom_call" | custom-call | flops 68719476736 | bytes 8388608 | tf_op jit(solution)/shard_map/pallas_call | solution.py:355
  284.2 5.0 %gather_fusion.1 = bf16[32,256,256]{2,1,0:T(8,128)(2,1)} fusion(bf16[32,256,256]{2,1,0:T(8,128)(2,1)} %bitcast.10, s32[1024]{0:T(1024)S(1)} %pad_clamp_fusion), kind=kCustom, calls=%fused_computation.1 | custom fusion | bytes 8388736 | tf_op jit(solution)/shard_map/gather | solution.py:378
  (2 shorter events, 0.0 us)

commit v2 on v1

--- a/solution.py
+++ b/solution.py
@@ -53,7 +53,7 @@
 
 def product_kernel(
     slots, half, width, mixing_ref, ordered_ref, out_ref,
-    left, own, oth, xo, yn, dt, own2, oth2, xo2, yn2, dt2,
+    left, panel, xo, yn, dt, own2, oth2, xo2, yn2, dt2,
     z_send, z_recv, in_sem, send_sems, recv_sems, p_send, p_recv, out_sem,
 ):
     tile = half // 2
@@ -73,6 +73,9 @@
     def others(k):
         return (z + k) % slots
 
+    own = panel.at[:, pl.ds(0, rows)]
+    oth = panel.at[:, pl.ds(rows, rows)]
+
     barrier = pltpu.get_barrier_semaphore()
     for k in range(1, slots):
         pl.semaphore_signal(barrier, inc=1, device_id={"inner": others(k)}, device_id_type=MESH)
@@ -151,40 +154,38 @@
 
     def put_same(source, s):
         def step(g, carry):
-            left[base0 + s, group(g), :] = source[s, group(g), :]
+            left[group(g), group(base0 + s)] = source[s, group(g), :]
             return carry
         lax.fori_loop(0, half, step, 0)
 
         def flip(g, carry):
-            left[base1 + g, group(base0 + s), :] = source[s, group(base1 + g), :].T
+            left[group(base0 + s), group(base1 + g)] = source[s, group(base1 + g), :].T
             return carry
         lax.fori_loop(0, tile, flip, 0)
 
     def put_dt(source, s):
         def step(g, carry):
-            left[base1 + s, group(base1 + g), :] = source[s, group(g), :]
+            left[group(base1 + g), group(base1 + s)] = source[s, group(g), :]
             return carry
         lax.fori_loop(0, tile, step, 0)
 
     def put_flipped(source, s, base):
         def step(g, carry):
-            left[half + g, group(base + s), :] = source[s, group(g), :].T
+            left[group(base + s), group(half + g)] = source[s, group(g), :].T
             return carry
         lax.fori_loop(0, half, step, 0)
 
     def put_plain(source, s, base):
         def step(g, carry):
-            left[half + base + s, group(g), :] = source[s, group(g), :]
+            left[group(g), group(half + base + s)] = source[s, group(g), :]
             return carry
         lax.fori_loop(0, half, step, 0)
 
     chunk = rows // 4
 
-    def multiply(right0, right1, s, row_start):
+    def multiply(s, row_start):
         here = pl.ds(pl.multiple_of(row_start, chunk), chunk)
-        lhs = jnp.concatenate([left[k, here, :] for k in range(2 * half)], axis=1)
-        rhs = jnp.concatenate([right0[s], right1[s]], axis=0)
-        return jnp.dot(lhs, rhs, preferred_element_type=jnp.float32).astype(jnp.bfloat16)
+        return jnp.dot(left[here, :], panel[s], preferred_element_type=jnp.float32).astype(jnp.bfloat16)
 
     link = links(0)
     order = [z, z + 1 - 2 * (z % 2), (z + 2) % 4, 3 - z] if slots == 4 else [others(k) for k in range(slots)]
@@ -222,41 +223,39 @@
     relay_and_put(order[-1])
 
     link2 = links(1)
-
-    def square_slot(s, carry):
-        def step(m, carry):
-            here = pl.ds(pl.multiple_of(m * chunk, chunk), chunk)
-            own2[s, here, :] = multiply(own, oth, s, m * chunk)
-            return carry
-        lax.fori_loop(0, rows // chunk, step, 0)
-        send_first(link2, s)
-        return carry
-
-    lax.fori_loop(0, slots, square_slot, 0)
-
-    for k in range(1, slots):
-        z_copy(k).wait_send()
     for s in range(slots):
         wait_sends(link, s)
-
     a, b, q = mixing_ref[0], mixing_ref[1], mixing_ref[2]
     eye = (
         lax.broadcasted_iota(jnp.int32, (width, width), 0) == lax.broadcasted_iota(jnp.int32, (width, width), 1)
     ).astype(jnp.float32)
 
+    def combine(dense, square):
+        return b * dense.astype(jnp.float32) + q * square.astype(jnp.float32)
+
     def mix(dense, square, s, holds_diag):
         def step(g, carry):
             scale = jnp.where(jnp.logical_and(holds_diag, g == base0 + s), a, 0.0)
             dense[s, group(g), :] = (
-                scale * eye
-                + b * dense[s, group(g), :].astype(jnp.float32)
-                + q * square[s, group(g), :].astype(jnp.float32)
+                scale * eye + combine(dense[s, group(g), :], square[s, group(g), :])
             ).astype(jnp.bfloat16)
             return carry
         lax.fori_loop(0, half, step, 0)
 
-    for s in range(slots):
+    def square_slot(s, carry):
+        def step(m, carry):
+            here = pl.ds(pl.multiple_of(m * chunk, chunk), chunk)
+            own2[s, here, :] = multiply(s, m * chunk)
+            return carry
+        lax.fori_loop(0, rows // chunk, step, 0)
+        send_first(link2, s)
         mix(own, own2, s, diag)
+        return carry
+
+    lax.fori_loop(0, slots, square_slot, 0)
+
+    for k in range(1, slots):
+        z_copy(k).wait_send()
     for s in range(slots):
         link2["core"](s).wait_recv()
         mix(oth, oth2, s, jnp.logical_not(diag))
@@ -287,7 +286,7 @@
             m = first + i // slots
             s = i % slots
             here = pl.ds(pl.multiple_of(m * chunk, chunk), chunk)
-            staged[s, here, :] = multiply(own, oth, s, m * chunk)
+            staged[s, here, :] = multiply(s, m * chunk)
 
             @pl.when(s == z)
             def _():
@@ -358,8 +357,9 @@
         in_specs=[pl.BlockSpec(memory_space=pltpu.SMEM), pl.BlockSpec(memory_space=pl.ANY)],
         out_specs=pl.BlockSpec(memory_space=pl.ANY),
         scratch_shapes=[
-            pltpu.VMEM((2 * half, rows, width), jnp.bfloat16),
-            panel, panel, panel, panel, part,
+            pltpu.VMEM((rows, 2 * rows), jnp.bfloat16),
+            pltpu.VMEM((slots, 2 * rows, width), jnp.bfloat16),
+            panel, panel, part,
             panel, panel, panel, panel, part,
             dma((slots,)), dma((slots,)), dma, dma((2, 4, slots)), dma((2, 4, slots)),
             dma((slots, 4)), dma((slots, 4)), dma((4,)),

time: 290 us -> 291 us (level)
  no operation moved by 1% of the time
where the time goes in v2:
time: 291 us; the launch traced here: 290 us
  Pallas kernels  278 us (96%)
  local copies, waits for them, and re-layouts  10.9 us (4%)
    pallas_call x1, Pallas kernels, plane_filter(): pl.pallas_call(functools.partial(product_kernel, slots, half, width), out...  278 us

profile of v2, /device:TPU:12, one launch (start us, length us, event | category | flops | bytes accessed | tf_op | source)
XLA Modules:
  0.0 289.6 jit_solution(10254731148071783570)
XLA Ops:
  0.0 0.7 slice.7
  0.7 0.7 dynamic-slice_subtract_fusion
  1.4 0.1 copy.4
  1.5 0.1 reshape.93
  1.6 0.1 fusion
  1.7 5.0 %gather_fusion = bf16[32,256,256]{2,1,0:T(8,128)(2,1)} fusion(bf16[32,256,256]{2,1,0:T(8,128)(2,1)} %bitcast.9, s32[1024]{0:T(1024)S(1)} %pad_clamp_fusion.1), kind=kCustom, calls=%fused_computation | custom fusion | bytes 8388736 | tf_op jit(solution)/shard_map/gather | solution.py:348
  6.7 277.9 %shard_map.37 = bf16[4,2048,256]{2,1,0:T(8,128)(2,1)} custom-call(f32[3]{0:T(128)} %mixing_ref.1, bf16[4,2048,256]{2,1,0:T(8,128)(2,1)} %bitcast.11), custom_call_target="tpu_custom_call" | custom-call | flops 68719476736 | bytes 8388608 | tf_op jit(solution)/shard_map/pallas_call | solution.py:354
  284.6 5.0 %gather_fusion.1 = bf16[32,256,256]{2,1,0:T(8,128)(2,1)} fusion(bf16[32,256,256]{2,1,0:T(8,128)(2,1)} %bitcast.10, s32[1024]{0:T(1024)S(1)} %pad_clamp_fusion), kind=kCustom, calls=%fused_computation.1 | custom fusion | bytes 8388736 | tf_op jit(solution)/shard_map/gather | solution.py:378
  (2 shorter events, 0.0 us)

commit v3 on v2

--- a/solution.py
+++ b/solution.py
@@ -51,6 +51,14 @@
     return regrouped[positions]
 
 
+class Part:
+    def __init__(self, ref, rows):
+        self.ref, self.rows = ref, rows
+
+    def __getitem__(self, slot):
+        return self.ref.at[slot, self.rows]
+
+
 def product_kernel(
     slots, half, width, mixing_ref, ordered_ref, out_ref,
     left, panel, xo, yn, dt, own2, oth2, xo2, yn2, dt2,
@@ -88,34 +96,39 @@
             src_ref=src, dst_ref=dst, send_sem=send, recv_sem=recv, device_id=target, device_id_type=MESH
         )
 
+    order = [z, z + 1 - 2 * (z % 2), (z + slots // 2) % slots, slots - 1 - z]
+
     def z_copy(k):
-        to = others(k)
+        to = order[k]
         return remote(ordered_ref.at[to], own.at[z], z_send.at[k], z_recv.at[z], {"inner": to})
 
     def z_arrival(s):
         return remote(ordered_ref.at[s], own.at[s], z_send.at[0], z_recv.at[s], {"inner": s})
 
-    for k in range(1, slots):
-        z_copy(k).start()
+    z_copy(2).start()
+    z_copy(1).start()
     keep = pltpu.make_async_copy(ordered_ref.at[z], own.at[z], in_sem)
     keep.start()
 
     def links(phase):
         mine, oth_, xo_, yn_, dt_ = ((own, oth, xo, yn, dt), (own2, oth2, xo2, yn2, dt2))[phase]
-        diag_rows = pl.ds(pl.multiple_of(base0 * width, width), tile * width)
+        rows0 = pl.ds(pl.multiple_of(base0 * width, width), tile * width)
+        rows1 = pl.ds(pl.multiple_of(base1 * width, width), tile * width)
 
         def make(kind, index, src, dst, target):
             return lambda s: remote(
-                src(s), dst.at[s], send_sems.at[phase, index, s], recv_sems.at[phase, kind, s], target
+                src(s), dst[s], send_sems.at[phase, index, s], recv_sems.at[phase, kind, s], target
             )
 
         return dict(
-            core=make(0, 0, lambda s: mine.at[s], oth_, to_core),
-            xo=make(1, 1, lambda s: mine.at[s], xo_, to_x),
-            yn=make(2, 2, lambda s: mine.at[s], yn_, to_y),
-            dt=make(3, 3, lambda s: mine.at[s, diag_rows], dt_, to_x),
-            dt_y=make(3, 1, lambda s: dt_.at[s], dt_, to_y),
-            xo_relay=make(1, 2, lambda s: xo_.at[s], xo_, to_core),
+            core=make(0, 0, lambda s: mine.at[s], oth_.at, to_core),
+            xo0=make(1, 1, lambda s: mine.at[s, rows1], Part(xo_, rows1), to_x),
+            xo1=make(4, 3, lambda s: mine.at[s, rows0], Part(xo_, rows0), to_x),
+            yn=make(2, 2, lambda s: mine.at[s], yn_.at, to_y),
+            dt=make(3, 3, lambda s: mine.at[s, rows0], dt_.at, to_x),
+            dt_y=make(3, 1, lambda s: dt_.at[s], dt_.at, to_y),
+            xo0_relay=make(1, 2, lambda s: xo_.at[s, rows0], Part(xo_, rows0), to_core),
+            xo1_relay=make(4, 4, lambda s: xo_.at[s, rows1], Part(xo_, rows1), to_core),
         )
 
     def send_first(link, s):
@@ -127,7 +140,7 @@
 
         @pl.when(jnp.logical_not(diag))
         def _():
-            link["xo"](s).start()
+            link["xo0"](s).start()
             link["core"](s).start()
 
     def wait_sends(link, s):
@@ -138,16 +151,21 @@
 
         @pl.when(jnp.logical_not(diag))
         def _():
-            for name in ("xo", "core", "xo_relay"):
+            for name in ("xo0", "xo1", "core", "xo0_relay", "xo1_relay"):
                 link[name](s).wait_send()
 
     def relay_dt(link, s):
         link["dt"](s).wait_recv()
         link["dt_y"](s).start()
 
-    def relay_xo(link, s):
-        link["xo"](s).wait_recv()
-        link["xo_relay"](s).start()
+    def relay_xo(link, s, part):
+        link[("xo0", "xo1")[part]](s).wait_recv()
+        link[("xo0_relay", "xo1_relay")[part]](s).start()
+
+    def send_second(link, s):
+        @pl.when(jnp.logical_not(diag))
+        def _():
+            link["xo1"](s).start()
 
     def group(g):
         return pl.ds(pl.multiple_of(g * width, width), width)
@@ -175,11 +193,11 @@
             return carry
         lax.fori_loop(0, half, step, 0)
 
-    def put_plain(source, s, base):
+    def put_plain(source, s, base, first, count):
         def step(g, carry):
-            left[group(g), group(half + base + s)] = source[s, group(g), :]
-            return carry
-        lax.fori_loop(0, half, step, 0)
+            left[group(first + g), group(half + base + s)] = source[s, group(first + g), :]
+            return carry
+        lax.fori_loop(0, count, step, 0)
 
     chunk = rows // 4
 
@@ -188,7 +206,6 @@
         return jnp.dot(left[here, :], panel[s], preferred_element_type=jnp.float32).astype(jnp.bfloat16)
 
     link = links(0)
-    order = [z, z + 1 - 2 * (z % 2), (z + 2) % 4, 3 - z] if slots == 4 else [others(k) for k in range(slots)]
 
     def relay_and_put(s):
         @pl.when(diag)
@@ -198,14 +215,16 @@
             put_dt(dt, s)
             link["core"](s).wait_recv()
             put_flipped(oth, s, base0)
-            link["xo_relay"](s).wait_recv()
+            link["xo0_relay"](s).wait_recv()
+            link["xo1_relay"](s).wait_recv()
             put_flipped(xo, s, base1)
 
         @pl.when(jnp.logical_not(diag))
         def _():
-            relay_xo(link, s)
-            put_plain(own, s, base0)
-            put_plain(xo, s, base1)
+            relay_xo(link, s, 0)
+            relay_xo(link, s, 1)
+            put_plain(own, s, base0, 0, half)
+            put_plain(xo, s, base1, 0, half)
             link["yn"](s).wait_recv()
             put_same(yn, s)
             link["dt_y"](s).wait_recv()
@@ -216,8 +235,12 @@
         if k == 0:
             keep.wait()
         else:
+            if k == 2:
+                z_copy(2).wait_send()
+                z_copy(3).start()
             z_arrival(s).wait_recv()
         send_first(link, s)
+        send_second(link, s)
         if k:
             relay_and_put(order[k - 1])
     relay_and_put(order[-1])
@@ -253,8 +276,10 @@
         return carry
 
     lax.fori_loop(0, slots, square_slot, 0)
-
-    for k in range(1, slots):
+    for s in range(slots):
+        send_second(link2, s)
+
+    for k in (1, 3):
         z_copy(k).wait_send()
     for s in range(slots):
         link2["core"](s).wait_recv()
@@ -308,21 +333,25 @@
             relay_dt(link2, s)
             put_dt(dt2, s)
         for s in range(slots):
-            link2["xo_relay"](s).wait_recv()
+            link2["xo0_relay"](s).wait_recv()
+            link2["xo1_relay"](s).wait_recv()
             put_flipped(xo2, s, base1)
         filter_tile(base1)
 
     @pl.when(jnp.logical_not(diag))
     def _():
         for s in range(slots):
-            put_plain(own2, s, base0)
-        for s in range(slots):
-            relay_xo(link2, s)
-            put_plain(xo2, s, base1)
+            put_plain(own2, s, base0, 0, half)
+        for s in range(slots):
+            relay_xo(link2, s, 0)
+            put_plain(xo2, s, base1, base0, tile)
         for s in range(slots):
             link2["yn"](s).wait_recv()
             put_same(yn2, s)
         filter_tile(base0)
+        for s in range(slots):
+            relay_xo(link2, s, 1)
+            put_plain(xo2, s, base1, base1, tile)
         for s in range(slots):
             link2["dt_y"](s).wait_recv()
             put_dt(dt2, s)
@@ -361,7 +390,7 @@
             pltpu.VMEM((slots, 2 * rows, width), jnp.bfloat16),
             panel, panel, part,
             panel, panel, panel, panel, part,
-            dma((slots,)), dma((slots,)), dma, dma((2, 4, slots)), dma((2, 4, slots)),
+            dma((slots,)), dma((slots,)), dma, dma((2, 5, slots)), dma((2, 5, slots)),
             dma((slots, 4)), dma((slots, 4)), dma((4,)),
         ],
         compiler_params=pltpu.CompilerParams(

time: 291 us -> 248 us (0.85)
  Pallas kernels: 278 us -> 234 us
    pallas_call x1, Pallas kernels: 278 us -> 234 us  [plane_filter(): pl.pallas_call(functools.partial(product_kernel, slots, half, width), out...]
where the time goes in v3:
time: 248 us; the launch traced here: 246 us
  Pallas kernels  234 us (94%)
  local copies, waits for them, and re-layouts  10.9 us (4%)
    pallas_call x1, Pallas kernels, plane_filter(): pl.pallas_call(functools.partial(product_kernel, slots, half, width), out...  234 us
    gather x1, local copies, waits for them, and re-layouts, plane_filter(): ordered = density[:, 0][(leaders - row_start).reshape(-1)]  5.02 us
    gather x1, local copies, waits for them, and re-layouts, plane_filter(): return regrouped[positions]  5.02 us

profile of v3, /device:TPU:12, one launch (start us, length us, event | category | flops | bytes accessed | tf_op | source)
XLA Modules:
  0.0 246.1 jit_solution(17584950655103333536)
XLA Ops:
  0.0 0.7 slice.7
  0.7 0.7 dynamic-slice_subtract_fusion
  1.4 0.1 copy.4
  1.5 0.1 reshape.93
  1.6 0.1 fusion
  1.7 5.0 %gather_fusion = bf16[32,256,256]{2,1,0:T(8,128)(2,1)} fusion(bf16[32,256,256]{2,1,0:T(8,128)(2,1)} %bitcast.9, s32[1024]{0:T(1024)S(1)} %pad_clamp_fusion.1), kind=kCustom, calls=%fused_computation | custom fusion | bytes 8388736 | tf_op jit(solution)/shard_map/gather | solution.py:377
  6.7 234.4 %shard_map.37 = bf16[4,2048,256]{2,1,0:T(8,128)(2,1)} custom-call(f32[3]{0:T(128)} %mixing_ref.1, bf16[4,2048,256]{2,1,0:T(8,128)(2,1)} %bitcast.11), custom_call_target="tpu_custom_call" | custom-call | flops 68719476736 | bytes 8388608 | tf_op jit(solution)/shard_map/pallas_call | solution.py:383
  241.0 5.0 %gather_fusion.1 = bf16[32,256,256]{2,1,0:T(8,128)(2,1)} fusion(bf16[32,256,256]{2,1,0:T(8,128)(2,1)} %bitcast.10, s32[1024]{0:T(1024)S(1)} %pad_clamp_fusion), kind=kCustom, calls=%fused_computation.1 | custom fusion | bytes 8388736 | tf_op jit(solution)/shard_map/gather | solution.py:407
  (2 shorter events, 0.0 us)

commit v4 on v3

--- a/solution.py
+++ b/solution.py
@@ -96,17 +96,56 @@
             src_ref=src, dst_ref=dst, send_sem=send, recv_sem=recv, device_id=target, device_id_type=MESH
         )
 
-    order = [z, z + 1 - 2 * (z % 2), (z + slots // 2) % slots, slots - 1 - z]
-
-    def z_copy(k):
+    def rank_of(v, k):
+        return (v, v + 1 - 2 * (v % 2), (v + slots // 2) % slots, slots - 1 - v)[k]
+
+    def group(g):
+        return pl.ds(pl.multiple_of(g * width, width), width)
+
+    order = [rank_of(z, k) for k in range(slots)]
+    far_rows = pl.ds(pl.multiple_of(base1 * width, width), tile * width)
+
+    def z_pieces(k, act):
         to = order[k]
-        return remote(ordered_ref.at[to], own.at[z], z_send.at[k], z_recv.at[z], {"inner": to})
-
-    def z_arrival(s):
-        return remote(ordered_ref.at[s], own.at[s], z_send.at[0], z_recv.at[s], {"inner": s})
-
-    z_copy(2).start()
-    z_copy(1).start()
+        act(remote(
+            ordered_ref.at[to, far_rows], own.at[z, far_rows], z_send.at[k, slots], z_recv.at[z, slots], {"inner": to}
+        ))
+        for j in range(slots):
+            here = group(base0 + rank_of(to, j))
+            copy = remote(
+                ordered_ref.at[to, here], own.at[z, here], z_send.at[k, j], z_recv.at[z, j], {"inner": to}
+            )
+            if j >= k:
+                act(copy)
+            else:
+                pl.when(jnp.logical_not(diag))(functools.partial(act, copy))
+
+    def z_arrival(k):
+        s = order[k]
+        remote(
+            ordered_ref.at[s, far_rows], own.at[s, far_rows], z_send.at[k, slots], z_recv.at[s, slots], {"inner": s}
+        ).wait_recv()
+        for j in range(slots):
+            here = group(base0 + order[j])
+            copy = remote(ordered_ref.at[s, here], own.at[s, here], z_send.at[k, j], z_recv.at[s, j], {"inner": s})
+            if j >= k:
+                copy.wait_recv()
+            else:
+                pl.when(jnp.logical_not(diag))(copy.wait_recv)
+
+        @pl.when(diag)
+        def _():
+            for j in range(k):
+                panel[s, group(base0 + order[j]), :] = panel[order[j], group(base0 + s), :].T
+
+    def z_start(k):
+        z_pieces(k, lambda copy: copy.start())
+
+    def z_wait_send(k):
+        z_pieces(k, lambda copy: copy.wait_send())
+
+    z_start(2)
+    z_start(1)
     keep = pltpu.make_async_copy(ordered_ref.at[z], own.at[z], in_sem)
     keep.start()
 
@@ -167,9 +206,6 @@
         def _():
             link["xo1"](s).start()
 
-    def group(g):
-        return pl.ds(pl.multiple_of(g * width, width), width)
-
     def put_same(source, s):
         def step(g, carry):
             left[group(g), group(base0 + s)] = source[s, group(g), :]
@@ -236,9 +272,9 @@
             keep.wait()
         else:
             if k == 2:
-                z_copy(2).wait_send()
-                z_copy(3).start()
-            z_arrival(s).wait_recv()
+                z_wait_send(2)
+                z_start(3)
+            z_arrival(k)
         send_first(link, s)
         send_second(link, s)
         if k:
@@ -280,7 +316,7 @@
         send_second(link2, s)
 
     for k in (1, 3):
-        z_copy(k).wait_send()
+        z_wait_send(k)
     for s in range(slots):
         link2["core"](s).wait_recv()
         mix(oth, oth2, s, jnp.logical_not(diag))
@@ -390,7 +426,7 @@
             pltpu.VMEM((slots, 2 * rows, width), jnp.bfloat16),
             panel, panel, part,
             panel, panel, panel, panel, part,
-            dma((slots,)), dma((slots,)), dma, dma((2, 5, slots)), dma((2, 5, slots)),
+            dma((slots, slots + 1)), dma((slots, slots + 1)), dma, dma((2, 5, slots)), dma((2, 5, slots)),
             dma((slots, 4)), dma((slots, 4)), dma((4,)),
         ],
         compiler_params=pltpu.CompilerParams(

time: 248 us -> 241 us (0.972)
  Pallas kernels: 234 us -> 229 us
    pallas_call x1, Pallas kernels: 234 us -> 229 us  [plane_filter(): pl.pallas_call(functools.partial(product_kernel, slots, half, width), out...]
where the time goes in v4:
time: 241 us; the launch traced here: 240 us
  Pallas kernels  229 us (95%)
  local copies, waits for them, and re-layouts  10.9 us (5%)
    pallas_call x1, Pallas kernels, plane_filter(): pl.pallas_call(functools.partial(product_kernel, slots, half, width), out...  229 us
    gather x1, local copies, waits for them, and re-layouts, plane_filter(): ordered = density[:, 0][(leaders - row_start).reshape(-1)]  5.02 us
    gather x1, local copies, waits for them, and re-layouts, plane_filter(): return regrouped[positions]  5.02 us

profile of v4, /device:TPU:12, one launch (start us, length us, event | category | flops | bytes accessed | tf_op | source)
XLA Modules:
  0.0 240.4 jit_solution(6242986912002757274)
XLA Ops:
  0.0 0.7 slice.7
  0.7 0.7 dynamic-slice_subtract_fusion
  1.4 0.1 copy.4
  1.5 0.1 reshape.93
  1.6 0.1 fusion
  1.7 5.0 %gather_fusion = bf16[32,256,256]{2,1,0:T(8,128)(2,1)} fusion(bf16[32,256,256]{2,1,0:T(8,128)(2,1)} %bitcast.9, s32[1024]{0:T(1024)S(1)} %pad_clamp_fusion.1), kind=kCustom, calls=%fused_computation | custom fusion | bytes 8388736 | tf_op jit(solution)/shard_map/gather | solution.py:413
  6.7 228.7 %shard_map.37 = bf16[4,2048,256]{2,1,0:T(8,128)(2,1)} custom-call(f32[3]{0:T(128)} %mixing_ref.1, bf16[4,2048,256]{2,1,0:T(8,128)(2,1)} %bitcast.11), custom_call_target="tpu_custom_call" | custom-call | flops 68719476736 | bytes 8388608 | tf_op jit(solution)/shard_map/pallas_call | solution.py:419
  235.4 5.0 %gather_fusion.1 = bf16[32,256,256]{2,1,0:T(8,128)(2,1)} fusion(bf16[32,256,256]{2,1,0:T(8,128)(2,1)} %bitcast.10, s32[1024]{0:T(1024)S(1)} %pad_clamp_fusion), kind=kCustom, calls=%fused_computation.1 | custom fusion | bytes 8388736 | tf_op jit(solution)/shard_map/gather | solution.py:443
  (2 shorter events, 0.0 us)
